TPU v7x, 32 devices: a whole 2x2x4 slice. The times are simulated.
32 devices in a mesh: expert: 8 (over z, y), tensor: 4 (over x, core).
Axes of the slice: x: 2, y: 2, z: 4, core: 2. Of those that a mesh axis runs over, the one named last changes fastest.
Arguments:
- inputs: bfloat16 [8192, 768], P('expert'), may hold values from -6 to 6
- gain_attn: float32 [768], replicated, may hold values from 0.5 to 1.5
- gain_ffn: float32 [768], replicated, may hold values from 0.5 to 1.5
- weight_qkv: bfloat16 [3, 768, 768], P(None, None, 'tensor'), may hold values from -0.21875 to 0.21875
- weight_attn_out: bfloat16 [768, 768], P('tensor'), may hold values from -0.875 to 0.875
- rel_table: float32 [32, 12], P(None, 'tensor'), may hold values from -4 to 4
- weight_router: bfloat16 [768, 8], replicated, may hold values from -0.15625 to 0.15625
- weight_in: bfloat16 [8, 768, 3072], P('expert', None, 'tensor'), may hold values from -0.21875 to 0.21875
- weight_out: bfloat16 [8, 3072, 768], P('expert', 'tensor'), may hold values from -0.109375 to 0.109375
- routes: int32 [8192, 2], P('expert'), may hold values from 0 to 7, all different within a row; in each aligned block of 1024 rows (0 to 1023, 1024 to 2047, ...) at most 344 rows name the same one
- segments: int32 [8192], P('expert'), may hold values from 0 to 95, never falling along the last dimension, each value on 1 to 512 neighbouring positions
- cotangent: bfloat16 [8192, 768], P('expert', 'tensor'), may hold values from -6 to 6
Outputs:
- activations: bfloat16 [8192, 768], P('expert', 'tensor')
- grad_input: float32 [8192, 768], P('expert')
- grad_gain_attn: float32 [768], replicated
- grad_gain_ffn: float32 [768], replicated
- grad_weight_qkv: float32 [3, 768, 768], P(None, None, 'tensor')
- grad_weight_attn_out: float32 [768, 768], P('tensor')
- grad_rel_table: float32 [32, 12], P(None, 'tensor')
- grad_weight_router: float32 [768, 8], replicated
- grad_weight_in: float32 [8, 768, 3072], P('expert', None, 'tensor')
- grad_weight_out: float32 [8, 3072, 768], P('expert', 'tensor')
Inputs may be any that keep to these rules, and one draw needn't show every extreme that they name: Each row names 2 different experts. In the rows of one device (aligned blocks of 1024 rows) no expert is named by more than 344 routes, a bound that some block reaches. `segments`: document numbers never fall along the tokens; a document has 1 to 512 tokens, and one has exactly 512.
All inputs are finite; a program needn't handle non-finite values.
Results may differ from a plain program's by a relative error of at most 0.012.
The roundings to bfloat16 on the way count: a program that leaves them out, or rounds other values in their place, can miss the bound.
Values may be sent and summed in bfloat16 or wider, within the bound.
A program may use at most 256 MiB of HBM per device.

v0:
```python
import math

import jax
import jax.numpy as jnp
from jax import lax
from jax.sharding import PartitionSpec as P

BLOCK = 512
BUCKETS = 32


epsilon = 1e-06
negative = -1e30
highest = lax.Precision.HIGHEST


def far_limits(buckets):
    half_size = buckets // 2
    base_ratio = 256.0 / buckets
    return [
        int(math.ceil(half_size * base_ratio ** (step / half_size))) for step in range(1, half_size)
    ]


def bucket_of(distance, buckets):
    half_size = buckets // 2
    limits = jnp.array(far_limits(buckets), dtype=jnp.int32)
    far_bucket = half_size + jnp.sum((distance[..., None] >= limits).astype(jnp.int32), axis=-1)
    return jnp.where(distance < half_size, distance, far_bucket)


def block_onehot(offset, wide_count, buckets):
    distance = jnp.maximum(offset + jnp.arange(wide_count, dtype=jnp.int32), 0)
    return (
        bucket_of(distance, buckets)[:, None] == jnp.arange(buckets, dtype=jnp.int32)[None, :]
    ).astype(jnp.float32)


def block_bias(diagonal_values, row_count, col_count):
    head_count, wide_count = diagonal_values.shape
    pattern = jnp.concatenate(
        [
            diagonal_values[:, :col_count][:, ::-1],
            jnp.zeros((head_count, 1), diagonal_values.dtype),
            diagonal_values[:, col_count:][:, ::-1],
        ],
        axis=1,
    )
    repeated = jnp.tile(pattern, (1, row_count))[:, : row_count * wide_count]
    return repeated.reshape(head_count, row_count, wide_count)[:, :, :col_count]


def block_allowed(positions, segments, row_start, key_len):
    return (positions[None, :key_len] <= positions[row_start:key_len, None]) & (
        segments[row_start:key_len, None] == segments[None, :key_len]
    )


def gather_diagonals(grid, row_count, col_count):
    head_count = grid.shape[0]
    wide_count = row_count + col_count - 1
    flipped = jnp.pad(grid[:, :, ::-1], ((0, 0), (0, 0), (0, row_count)))
    flat_rows = flipped.reshape(head_count, row_count * (row_count + col_count))[
        :, : row_count * wide_count
    ]
    return jnp.sum(flat_rows.reshape(head_count, row_count, wide_count), axis=1, dtype=jnp.float32)


def block_scores(query_block, key_block, bias_block, allowed, score_scale):
    scores = (
        jnp.einsum("qhd,khd->hqk", query_block, key_block, preferred_element_type=jnp.float32)
        * score_scale
        + bias_block
    )
    return jnp.where(allowed[None], scores, negative)


def norm_back(row_grads, unit_rows, root_rows, gain_vector):
    unit_grads = row_grads * gain_vector
    return root_rows * (
        unit_grads - unit_rows * jnp.mean(unit_grads * unit_rows, axis=-1, keepdims=True)
    )


def per_device(
    inputs,
    gain_attn,
    gain_ffn,
    weight_qkv,
    weight_attn_out,
    rel_table,
    weight_router,
    weight_in,
    weight_out,
    routes,
    segments,
    cotangent,
):
    seq_len, width = inputs.shape
    heads_local = rel_table.shape[1]
    col_width = weight_qkv.shape[2]
    head_size = col_width // heads_local
    score_scale = head_size ** (-0.5)
    block_rows = min(BLOCK, seq_len)
    block_count = seq_len // block_rows
    experts = weight_router.shape[1]
    local_experts = weight_in.shape[0]
    source_count = experts // local_experts
    top_count = routes.shape[1]
    capacity = (4 * seq_len * top_count + 24 * experts - 1) // (24 * experts) * 8
    out_width = cotangent.shape[1]
    column_start = lax.axis_index("tensor") * out_width
    stream_in = inputs.astype(jnp.float32)
    root_attn = lax.rsqrt(jnp.mean(stream_in * stream_in, axis=-1, keepdims=True) + epsilon)
    unit_attn = stream_in * root_attn
    normed_attn = (unit_attn * gain_attn).astype(jnp.bfloat16)
    projected = jnp.einsum(
        "td,kdc->ktc", normed_attn, weight_qkv, preferred_element_type=jnp.float32
    ).astype(jnp.bfloat16)
    queries = projected[0].reshape(seq_len, heads_local, head_size)
    keys_all = projected[1].reshape(seq_len, heads_local, head_size)
    values_all = projected[2].reshape(seq_len, heads_local, head_size)
    positions = jnp.arange(seq_len, dtype=jnp.int32)
    onehot_list, diagonal_list, log_sums, mixed_parts = ([], [], [], [])
    for which_block in range(block_count):
        row_start = which_block * block_rows
        key_len = row_start + block_rows
        wide_count = block_rows + key_len - 1
        onehot_block = block_onehot(row_start - (key_len - 1), wide_count, BUCKETS)
        allowed = block_allowed(positions, segments, row_start, key_len)
        diagonal_values = jnp.einsum("bh,wb->hw", rel_table, onehot_block, precision=highest)
        bias_block = block_bias(diagonal_values, block_rows, key_len)
        scores = block_scores(
            queries[row_start:key_len], keys_all[:key_len], bias_block, allowed, score_scale
        )
        row_peak = jnp.max(scores, axis=-1, keepdims=True)
        exp_scores = jnp.exp(scores - row_peak)
        row_total = jnp.sum(exp_scores, axis=-1, keepdims=True)
        probs_low = (exp_scores / row_total).astype(jnp.bfloat16)
        mixed_parts.append(
            jnp.einsum(
                "hqk,khd->qhd", probs_low, values_all[:key_len], preferred_element_type=jnp.float32
            )
        )
        log_sums.append(row_peak + jnp.log(row_total))
        onehot_list.append(onehot_block)
        diagonal_list.append(diagonal_values)
    mixed_heads = (
        jnp.concatenate(mixed_parts, axis=0).reshape(seq_len, col_width).astype(jnp.bfloat16)
    )
    attn_part = jnp.dot(mixed_heads, weight_attn_out, preferred_element_type=jnp.float32)
    attn_total = lax.psum(attn_part, "tensor")
    stream_mid = stream_in + attn_total
    root_ffn = lax.rsqrt(jnp.mean(stream_mid * stream_mid, axis=-1, keepdims=True) + epsilon)
    unit_ffn = stream_mid * root_ffn
    normed_ffn = (unit_ffn * gain_ffn).astype(jnp.bfloat16)
    logits = jnp.dot(normed_ffn, weight_router, preferred_element_type=jnp.float32)
    expert_ids = jnp.arange(experts, dtype=jnp.int32)
    route_hot = routes[:, :, None] == expert_ids[None, None, :]
    chosen = jnp.sum(jnp.where(route_hot, logits[:, None, :], 0.0), axis=-1)
    gate_weights = jax.nn.softmax(chosen, axis=-1)
    route_flat = routes.reshape(-1)
    route_count = route_flat.shape[0]
    flat_hot = (route_flat[:, None] == expert_ids[None, :]).astype(jnp.int32)
    earlier = jnp.cumsum(flat_hot, axis=0) - flat_hot
    slot_rank = jnp.sum(earlier * flat_hot, axis=1)
    slot_index = route_flat * capacity + slot_rank
    slot_route = (
        jnp.full((experts * capacity,), route_count, jnp.int32)
        .at[slot_index]
        .set(jnp.arange(route_count, dtype=jnp.int32))
    )
    slot_token = jnp.where(slot_route < route_count, slot_route // top_count, seq_len)
    padded_rows = jnp.concatenate([normed_ffn, jnp.zeros((1, width), jnp.bfloat16)], axis=0)
    sent_rows = padded_rows[slot_token].reshape(experts, capacity, width)
    arrived = lax.all_to_all(sent_rows, "expert", split_axis=0, concat_axis=0, tiled=True)
    arrived = arrived.reshape(source_count, local_experts, capacity, width)
    hidden_pre = jnp.einsum(
        "nlcd,ldf->nlcf", arrived, weight_in, preferred_element_type=jnp.float32
    )
    hidden = jax.nn.gelu(hidden_pre).astype(jnp.bfloat16)
    expert_part = jnp.einsum(
        "nlcf,lfd->nlcd", hidden, weight_out, preferred_element_type=jnp.float32
    )
    expert_share = lax.psum_scatter(expert_part, "tensor", scatter_dimension=3, tiled=True).astype(
        jnp.bfloat16
    )
    returned = lax.all_to_all(
        expert_share.reshape(experts, capacity, out_width),
        "expert",
        split_axis=0,
        concat_axis=0,
        tiled=True,
    )
    picked = (
        returned.reshape(experts * capacity, out_width)[slot_index]
        .astype(jnp.float32)
        .reshape(seq_len, top_count, out_width)
    )
    combined = jnp.sum(gate_weights[:, :, None] * picked, axis=1)
    activations = (
        lax.dynamic_slice_in_dim(stream_mid, column_start, out_width, 1) + combined
    ).astype(jnp.bfloat16)
    out_grad = cotangent.astype(jnp.float32)
    gate_part = jnp.sum(out_grad[:, None, :] * picked, axis=-1)
    slot_grads = (
        (gate_weights[:, :, None] * out_grad[:, None, :])
        .astype(jnp.bfloat16)
        .reshape(route_count, out_width)
    )
    slot_grads = jnp.concatenate([slot_grads, jnp.zeros((1, out_width), jnp.bfloat16)], axis=0)[
        slot_route
    ]
    result_grads = lax.all_to_all(
        slot_grads.reshape(experts, capacity, out_width),
        "expert",
        split_axis=0,
        concat_axis=0,
        tiled=True,
    )
    result_grads = lax.all_gather(
        result_grads.reshape(source_count, local_experts, capacity, out_width),
        "tensor",
        axis=3,
        tiled=True,
    )
    hidden_grads = jnp.einsum(
        "nlcd,lfd->nlcf", result_grads, weight_out, preferred_element_type=jnp.float32
    )
    grad_weight_out = jnp.einsum(
        "nlcf,nlcd->lfd", hidden, result_grads, preferred_element_type=jnp.float32
    )
    gelu_back = jax.vjp(jax.nn.gelu, hidden_pre)[1]
    pre_grads = gelu_back(hidden_grads)[0].astype(jnp.bfloat16)
    grad_weight_in = jnp.einsum(
        "nlcd,nlcf->ldf", arrived, pre_grads, preferred_element_type=jnp.float32
    )
    row_part = jnp.einsum(
        "nlcf,ldf->nlcd", pre_grads, weight_in, preferred_element_type=jnp.float32
    )
    row_share = lax.psum_scatter(row_part, "tensor", scatter_dimension=3, tiled=True).astype(
        jnp.bfloat16
    )
    row_back = lax.all_to_all(
        row_share.reshape(experts, capacity, out_width),
        "expert",
        split_axis=0,
        concat_axis=0,
        tiled=True,
    )
    normed_part = jnp.sum(
        row_back.reshape(experts * capacity, out_width)[slot_index]
        .astype(jnp.float32)
        .reshape(seq_len, top_count, out_width),
        axis=1,
    )
    gate_grads = lax.psum(gate_part, "tensor")
    chosen_grads = gate_weights * (
        gate_grads - jnp.sum(gate_weights * gate_grads, axis=-1, keepdims=True)
    )
    logit_grads = jnp.sum(jnp.where(route_hot, chosen_grads[:, :, None], 0.0), axis=1).astype(
        jnp.bfloat16
    )
    grad_weight_router = jnp.einsum(
        "td,te->de", normed_ffn, logit_grads, preferred_element_type=jnp.float32
    )
    router_back = jnp.einsum(
        "te,de->td", logit_grads, weight_router, preferred_element_type=jnp.float32
    )
    normed_grads, stream_grads = (
        lax.all_gather(normed_part, "tensor", axis=1, tiled=True),
        lax.all_gather(out_grad, "tensor", axis=1, tiled=True),
    )
    normed_grads = normed_grads + router_back
    grad_gain_ffn = jnp.sum(normed_grads * unit_ffn, axis=0)
    mid_grads = stream_grads + norm_back(normed_grads, unit_ffn, root_ffn, gain_ffn)
    attn_grads = mid_grads.astype(jnp.bfloat16)
    grad_weight_attn_out = jnp.einsum(
        "tc,td->cd", mixed_heads, attn_grads, preferred_element_type=jnp.float32
    )
    mixed_grads = jnp.einsum(
        "td,cd->tc", attn_grads, weight_attn_out, preferred_element_type=jnp.float32
    )
    mixed_grads = mixed_grads.astype(jnp.bfloat16).reshape(seq_len, heads_local, head_size)
    key_grads = jnp.zeros((seq_len, heads_local, head_size), jnp.float32)
    value_grads = jnp.zeros((seq_len, heads_local, head_size), jnp.float32)
    table_grad = jnp.zeros((BUCKETS, heads_local), jnp.float32)
    query_parts = []
    for which_block in range(block_count):
        row_start = which_block * block_rows
        key_len = row_start + block_rows
        allowed = block_allowed(positions, segments, row_start, key_len)
        bias_block = block_bias(diagonal_list[which_block], block_rows, key_len)
        scores = block_scores(
            queries[row_start:key_len], keys_all[:key_len], bias_block, allowed, score_scale
        )
        attn_probs = jnp.exp(scores - log_sums[which_block])
        probs_low = attn_probs.astype(jnp.bfloat16)
        grad_rows = mixed_grads[row_start:key_len]
        prob_grads = jnp.einsum(
            "qhd,khd->hqk", grad_rows, values_all[:key_len], preferred_element_type=jnp.float32
        )
        value_part = jnp.einsum(
            "hqk,qhd->khd", probs_low, grad_rows, preferred_element_type=jnp.float32
        )
        value_grads = value_grads + jnp.pad(value_part, ((0, seq_len - key_len), (0, 0), (0, 0)))
        row_dots = jnp.sum(attn_probs * prob_grads, axis=-1, keepdims=True)
        score_grads = (attn_probs * (prob_grads - row_dots)).astype(jnp.bfloat16)
        query_parts.append(
            jnp.einsum(
                "hqk,khd->qhd", score_grads, keys_all[:key_len], preferred_element_type=jnp.float32
            )
            * score_scale
        )
        key_part = (
            jnp.einsum(
                "hqk,qhd->khd",
                score_grads,
                queries[row_start:key_len],
                preferred_element_type=jnp.float32,
            )
            * score_scale
        )
        key_grads = key_grads + jnp.pad(key_part, ((0, seq_len - key_len), (0, 0), (0, 0)))
        diagonal_grads = gather_diagonals(score_grads, block_rows, key_len)
        table_grad = table_grad + jnp.einsum(
            "hw,wb->bh", diagonal_grads, onehot_list[which_block], precision=highest
        )
    qkv_grads = jnp.stack(
        [
            jnp.concatenate(query_parts, axis=0).reshape(seq_len, col_width),
            key_grads.reshape(seq_len, col_width),
            value_grads.reshape(seq_len, col_width),
        ],
        axis=0,
    ).astype(jnp.bfloat16)
    grad_weight_qkv = jnp.einsum(
        "td,ktc->kdc", normed_attn, qkv_grads, preferred_element_type=jnp.float32
    )
    normed_attn_part = jnp.einsum(
        "ktc,kdc->td", qkv_grads, weight_qkv, preferred_element_type=jnp.float32
    )
    normed_attn_grads = lax.psum(normed_attn_part, "tensor")
    grad_gain_attn = jnp.sum(normed_attn_grads * unit_attn, axis=0)
    grad_input = mid_grads + norm_back(normed_attn_grads, unit_attn, root_attn, gain_attn)
    shared = lax.psum(
        (
            grad_gain_attn,
            grad_gain_ffn,
            grad_weight_qkv,
            grad_weight_attn_out,
            table_grad,
            grad_weight_router,
        ),
        "expert",
    )
    return (
        activations,
        grad_input,
        shared[0],
        shared[1],
        shared[2],
        shared[3],
        shared[4],
        shared[5],
        grad_weight_in,
        grad_weight_out,
    )


def solution(mesh):
    in_specs = (
        P("expert", None),
        P(),
        P(),
        P(None, None, "tensor"),
        P("tensor", None),
        P(None, "tensor"),
        P(),
        P("expert", None, "tensor"),
        P("expert", "tensor", None),
        P("expert", None),
        P("expert"),
        P("expert", "tensor"),
    )
    out_specs = (
        P("expert", "tensor"),
        P("expert", None),
        P(),
        P(),
        P(None, None, "tensor"),
        P("tensor", None),
        P(None, "tensor"),
        P(),
        P("expert", None, "tensor"),
        P("expert", "tensor", None),
    )
    return jax.shard_map(
        per_device, mesh=mesh, in_specs=in_specs, out_specs=out_specs, check_vma=False
    )
```

profile of v0, /device:TPU:0, one launch (start us, length us, event | category | flops | bytes accessed | tf_op | source)
XLA Modules:
  0.0 927.0 jit_solution(18328193047216041508)
XLA Ops:
  35.0 13.2 %reshape.398 = f32[3,512,1023]{2,1,0:T(8,128)} reshape(f32[3,523776]{1,0:T(4,128)} %slice.161) | data formatting | bytes 12570624 | tf_op jit(solution)/shard_map/reshape | solution.py:50
  56.9 19.9 %copy.152 = f32[1,3,512,1536]{3,1,2,0:T(4,128)S(1)} copy(f32[1,3,512,1536]{3,2,1,0:T(8,128)S(1)} %broadcast_bitcast_fusion) | data formatting | bytes 18874368
  82.7 13.2 %reshape.474 = f32[2357760]{0:T(1024)} reshape(f32[3,785920]{1,0:T(4,128)} %slice.168) | data formatting | bytes 18862080
  95.9 16.1 %reshape.399 = f32[3,512,1535]{2,1,0:T(8,128)} reshape(f32[2357760]{0:T(1024)} %reshape.474) | data formatting | bytes 18862080 | tf_op jit(solution)/shard_map/reshape | solution.py:50
  149.7 50.5 %all-reduce.12.cloned.1.call-done = f32[1024,768]{1,0:T(8,128)} async-done(((f32[1024,768]{1,0:T(8,128)}), f32[1024,768]{1,0:T(8,128)}) %all-reduce.12.cloned.1.call-update) | async-done | bytes 3145744 | tf_op jit(solution)/shard_map/psum | solution.py:152
  226.2 9.3 %gather_fusion = bf16[2752,768]{1,0:T(8,128)(2,1)} fusion(bf16[1025,768]{1,0:T(8,128)(2,1)S(1)} %concatenate.25, s32[3072]{0:T(1024)S(1)} %get-tuple-element.106), kind=kCustom, calls=%fused_computation | custom fusion | bytes 8465152 | tf_op jit(solution)/shard_map/gather | solution.py:175
  235.5 17.7 %all-to-all-done.2 = bf16[8,344,192]{1,2,0:T(8,128)(2,1)} async-done(((bf16[8,344,192]{1,2,0:T(8,128)(2,1)}), bf16[8,344,192]{1,2,0:T(8,128)(2,1)}, u32[]{:S(2)}, u32[]{:S(2)}) %all-to-all-start.2) | async-done | bytes 1056800 | tf_op jit(solution)/shard_map/all_to_all | solution.py:214
  258.7 92.4 %all-to-all-done = bf16[8,344,768]{2,1,0:T(8,128)(2,1)} async-done(((bf16[8,344,768]{2,1,0:T(8,128)(2,1)}), bf16[8,344,768]{2,1,0:T(8,128)(2,1)}, u32[]{:S(2)}, u32[]{:S(2)}) %all-to-all-start) | async-done | bytes 4227104 | tf_op jit(solution)/shard_map/all_to_all | solution.py:176
  360.2 11.4 %fusion.6 = bf16[8,1,344,768]{3,2,0,1:T(8,128)(2,1)S(1)} fusion(f32[8,344,768]{2,1,0:T(8,128)} %fusion.80, bf16[8,344,768]{1,2,0:T(8,128)(2,1)} %all-gather.9.cloned.1.call-done, bf16[1,768,768]{2,1,0:T(8,128)(2,1)S(1)} %copy-done.55), kind=kOutput, calls=%fused_computation.13 | convolution fusion | flops 3288662016 | bytes 18087936 | tf_op jit(solution)/shard_map/nlcd,lfd->nlcf/dot_general | solution.py:227
  379.4 9.4 %copy.131 = f32[8,1,344,768]{2,0,1,3:T(8,128)} copy(f32[8,1,344,768]{3,2,0,1:T(8,128)} %fusion.29) | data formatting | bytes 16908288 | tf_op jit(solution)/shard_map/nlcf,ldf->nlcd/transpose | solution.py:238
  391.1 13.3 %fusion.26 = f32[8,1,344,768]{3,2,0,1:T(8,128)} fusion(bf16[1,768,768]{2,1,0:T(8,128)(2,1)S(1)} %copy-done.55, f32[8,344,768]{2,1,0:T(8,128)} %fusion.80), kind=kOutput, calls=%fused_computation.49 | convolution fusion | flops 3265413120 | bytes 18087936 | tf_op jit(solution)/shard_map/nlcf,lfd->nlcd/dot_general | solution.py:182
  404.4 9.9 %copy.124 = f32[8,1,344,768]{2,0,1,3:T(8,128)} copy(f32[8,1,344,768]{3,2,0,1:T(8,128)} %fusion.26) | data formatting | bytes 16908288 | tf_op jit(solution)/shard_map/nlcf,lfd->nlcd/transpose | solution.py:182
  414.3 51.5 %reduce-scatter.5.cloned.1.call-done = f32[8,1,344,192]{2,0,1,3:T(8,128)} async-done(((f32[8,1,344,768]{2,0,1,3:T(8,128)}), f32[8,1,344,192]{2,0,1,3:T(8,128)}) %reduce-scatter.5.cloned.1.call-update) | async-done | bytes 2113552 | tf_op jit(solution)/shard_map/reduce_scatter | solution.py:241
  474.4 28.5 %all-to-all-done.3 = bf16[8,344,192]{1,2,0:T(8,128)(2,1)S(1)} async-done(((bf16[8,344,192]{1,2,0:T(8,128)(2,1)}), bf16[8,344,192]{1,2,0:T(8,128)(2,1)S(1)}, u32[]{:S(2)}, u32[]{:S(2)}) %all-to-all-start.3) | async-done | bytes 1056800 | tf_op jit(solution)/shard_map/all_to_all | solution.py:244
  519.8 57.5 %reduce-scatter.3.cloned.1.call-done = f32[8,1,344,192]{2,0,1,3:T(8,128)} async-done(((f32[8,1,344,768]{2,0,1,3:T(8,128)}), f32[8,1,344,192]{2,0,1,3:T(8,128)}) %reduce-scatter.3.cloned.1.call-update) | async-done | bytes 2113552 | tf_op jit(solution)/shard_map/reduce_scatter | solution.py:185
  595.2 12.5 %fusion.46 = f32[1,768,768]{2,1,0:T(8,128)} fusion(bf16[8,344,768]{1,2,0:T(8,128)(2,1)} %all-gather.9.cloned.1.call-done, f32[8,344,768]{2,1,0:T(8,128)} %fusion.80), kind=kOutput, calls=%fused_computation.84 | convolution fusion | flops 3265413120 | bytes 15040512 | tf_op jit(solution)/shard_map/nlcf,nlcd->lfd/dot_general | solution.py:230
  626.6 9.1 multiply_reduce_fusion.5
  670.2 47.8 %rev.27 = bf16[3,512,1024]{2,1,0:T(8,128)(2,1)} reverse(bf16[3,512,1024]{2,1,0:T(8,128)(2,1)} %copy-done.7), dimensions={2} | reverse | bytes 6291456 | tf_op jit(solution)/shard_map/rev | solution.py:62
  743.0 15.3 %rev.26 = bf16[3,512,512]{1,2,0:T(8,128)(2,1)} reverse(bf16[3,512,512]{1,2,0:T(8,128)(2,1)S(1)} %multiply_convert_fusion.1), dimensions={2} | reverse | bytes 3145728 | tf_op jit(solution)/shard_map/rev | solution.py:62
  775.6 13.3 %reshape.417 = f32[3,512,1023]{2,1,0:T(8,128)} reshape(f32[3,523776]{1,0:T(4,128)} %slice_convert_fusion.1) | data formatting | bytes 12570624 | tf_op jit(solution)/shard_map/convert_element_type | solution.py:66
  792.2 13.4 %reshape.476 = f32[2357760]{0:T(1024)} reshape(f32[3,785920]{1,0:T(4,128)} %slice_convert_fusion) | data formatting | bytes 18862080
  805.6 15.7 %reshape.418 = f32[3,512,1535]{2,1,0:T(8,128)} reshape(f32[2357760]{0:T(1024)} %reshape.476) | data formatting | bytes 18862080 | tf_op jit(solution)/shard_map/convert_element_type | solution.py:66
  829.3 37.4 %all-reduce.6 = (f32[768]{0:T(1024)}, f32[768]{0:T(1024)}, f32[32,3]{0,1:T(4,128)}, f32[768,8]{0,1:T(8,128)}) all-reduce(f32[768]{0:T(1024)S(1)} %get-tuple-element.72, f32[768]{0:T(1024)S(1)} %get-tuple-element.70, f32[32,3]{0,1:T(4,128)S(1)} %convolution_add_fusion.1, ...), channel_id=1, replica_groups=mesh['expert'=8,'tensor'=4] {'expert'}, use_global_device_ids=true, to_apply=%region_30.31 | all-reduce | flops 7776 | bytes 62208 | tf_op jit(solution)/shard_map/psum | solution.py:346
  872.2 44.0 %all-reduce.16.cloned.1.call-done = (f32[3,768,192]{1,2,0:T(8,128)}, f32[192,768]{1,0:T(8,128)}) async-done(((f32[3,768,192]{1,2,0:T(8,128)}, f32[192,768]{1,0:T(8,128)}), (f32[3,768,192]{1,2,0:T(8,128)}, f32[192,768]{1,0:T(8,128)})) %all-reduce.16.cloned.1.call-update) | async-done | bytes 2359312 | tf_op jit(solution)/shard_map/psum | solution.py:346
  (306 shorter events, 289.1 us)
Async XLA Ops:
  7.2 343.9 %copy-start = (bf16[1,768,768]{2,1,0:T(8,128)(2,1)S(1)}, bf16[1,768,768]{2,1,0:T(8,128)(2,1)}, u32[]{:S(2)}) copy-start(bf16[1,768,768]{2,1,0:T(8,128)(2,1)} %param.21) | copy-start | bytes 3538948
  7.2 193.0 %all-reduce.12.cloned.1.call-start = ((), (), s32[]{:S(2)}) async-start(), calls=%async_computation.6 | async-start | bytes 6291456 | tf_op jit(solution)/shard_map/psum | solution.py:152
  9.2 6.8 copy-start.47
  17.1 100.5 %copy-start.23 = (bf16[1,512,192]{1,2,0:T(8,128)(2,1)}, bf16[1,512,192]{1,2,0:T(8,128)(2,1)S(1)}, u32[]{:S(2)}) copy-start(bf16[1,512,192]{1,2,0:T(8,128)(2,1)S(1)} %get-tuple-element.85) | copy-start | bytes 589828
  95.9 16.1 %slice-start.9 = ((s32[1024]{0:T(1024)}), s32[512]{0:T(512)S(1)}, s32[]{:S(2)}) async-start(s32[1024]{0:T(1024)} %copy-done.48), calls=%async_computation.23 | async-start | bytes 4096 | tf_op jit(solution)/shard_map/slice | solution.py:54
  95.9 16.9 %copy-start.25 = (bf16[1,512,192]{1,2,0:T(8,128)(2,1)S(1)}, bf16[1,512,192]{1,2,0:T(8,128)(2,1)}, u32[]{:S(2)}) copy-start(bf16[1,512,192]{1,2,0:T(8,128)(2,1)} %get-tuple-element.86) | copy-start | bytes 589828
  95.9 16.9 %copy-start.27 = (bf16[1,512,192]{1,2,0:T(8,128)(2,1)S(1)}, bf16[1,512,192]{1,2,0:T(8,128)(2,1)}, u32[]{:S(2)}) copy-start(bf16[1,512,192]{1,2,0:T(8,128)(2,1)} %get-tuple-element.84) | copy-start | bytes 589828
  134.2 66.0 %copy-start.13 = (bf16[1024,768]{1,0:T(8,128)(2,1)S(1)}, bf16[1024,768]{1,0:T(8,128)(2,1)}, u32[]{:S(2)}) copy-start(bf16[1024,768]{1,0:T(8,128)(2,1)} %param.14) | copy-start | bytes 4718596
  149.7 52.9 %copy-start.44 = (f32[768]{0:T(1024)S(1)}, f32[768]{0:T(1024)}, u32[]{:S(2)}) copy-start(f32[768]{0:T(1024)} %param.16) | copy-start | bytes 9220
  219.2 34.1 %all-to-all-start.2 = ((bf16[8,344,192]{1,2,0:T(8,128)(2,1)}), bf16[8,344,192]{1,2,0:T(8,128)(2,1)}, u32[]{:S(2)}, u32[]{:S(2)}) async-start(bf16[8,344,192]{1,2,0:T(8,128)(2,1)} %copy.130), calls=%async_computation.3 | async-start | bytes 2359296 | tf_op jit(solution)/shard_map/all_to_all | solution.py:214
  253.3 97.8 %all-to-all-start = ((bf16[8,344,768]{2,1,0:T(8,128)(2,1)}), bf16[8,344,768]{2,1,0:T(8,128)(2,1)}, u32[]{:S(2)}, u32[]{:S(2)}) async-start(bf16[8,344,768]{2,1,0:T(8,128)(2,1)} %bitcast.236), calls=%async_computation | async-start | bytes 8454144 | tf_op jit(solution)/shard_map/all_to_all | solution.py:176
  257.9 102.3 %all-gather.9.cloned.1.call-start = ((), (), s32[]{:S(2)}) async-start(), calls=%async_computation.12 | async-start | bytes 5898240 | tf_op jit(solution)/shard_map/all_gather | solution.py:221
  258.6 101.6 %copy-start.55 = (bf16[1,768,768]{2,1,0:T(8,128)(2,1)S(1)}, bf16[1,768,768]{2,1,0:T(8,128)(2,1)}, u32[]{:S(2)}) copy-start(bf16[1,768,768]{2,1,0:T(8,128)(2,1)} %param.22) | copy-start | bytes 3538948
  258.6 207.2 %reduce-scatter.5.cloned.1.call-start = ((), (), s32[]{:S(2)}) async-start(), calls=%async_computation.9 | async-start | bytes 11796480 | tf_op jit(solution)/shard_map/reduce_scatter | solution.py:241
  388.8 127.3 %all-gather.5.cloned.1.call-start = ((), (), s32[]{:S(2)}) async-start(), calls=%async_computation.8 | async-start | bytes 3932160 | tf_op jit(solution)/shard_map/all_gather | solution.py:272
  390.8 186.5 %reduce-scatter.3.cloned.1.call-start = ((), (), s32[]{:S(2)}) async-start(), calls=%async_computation.7 | async-start | bytes 11796480 | tf_op jit(solution)/shard_map/reduce_scatter | solution.py:185
  468.8 34.1 %all-to-all-start.3 = ((bf16[8,344,192]{1,2,0:T(8,128)(2,1)}), bf16[8,344,192]{1,2,0:T(8,128)(2,1)S(1)}, u32[]{:S(2)}, u32[]{:S(2)}) async-start(bf16[8,344,192]{1,2,0:T(8,128)(2,1)} %copy.132), calls=%async_computation.5 | async-start | bytes 2359296 | tf_op jit(solution)/shard_map/all_to_all | solution.py:244
  474.3 172.9 %all-gather.7.cloned.1.call-start = ((), (), s32[]{:S(2)}) async-start(), calls=%async_computation.10 | async-start | bytes 3932160 | tf_op jit(solution)/shard_map/all_gather | solution.py:271
  580.3 34.1 %all-to-all-start.1 = ((bf16[8,344,192]{1,2,0:T(8,128)(2,1)}), bf16[8,344,192]{1,2,0:T(8,128)(2,1)S(1)}, u32[]{:S(2)}, u32[]{:S(2)}) async-start(bf16[8,344,192]{1,2,0:T(8,128)(2,1)} %copy.125), calls=%async_computation.2 | async-start | bytes 2359296 | tf_op jit(solution)/shard_map/all_to_all | solution.py:188
  585.8 240.6 %all-reduce.14.cloned.1.call-start = ((), (), s32[]{:S(2)}) async-start(), calls=%async_computation.11 | async-start | bytes 6291456 | tf_op jit(solution)/shard_map/psum | solution.py:343
  635.7 10.5 %copy-start.12 = (bf16[1024,768]{1,0:T(8,128)(2,1)S(1)}, bf16[1024,768]{1,0:T(8,128)(2,1)}, u32[]{:S(2)}) copy-start(bf16[1024,768]{1,0:T(8,128)(2,1)} %copy-done.11) | copy-start | bytes 4718596
  722.1 9.2 copy-start.38
  734.4 181.8 %all-reduce.16.cloned.1.call-start = ((), (), s32[]{:S(2)}) async-start(), calls=%async_computation.13 | async-start | bytes 4718592 | tf_op jit(solution)/shard_map/psum | solution.py:346
  866.7 53.2 %copy-start.1 = (bf16[1,768,768]{2,1,0:T(8,128)(2,1)S(1)}, bf16[1,768,768]{2,1,0:T(8,128)(2,1)}, u32[]{:S(2)}) copy-start(bf16[1,768,768]{2,1,0:T(8,128)(2,1)} %param.21) | copy-start | bytes 3538948
  (56 other events, 158.3 us)
Sparse Core Ops, SparseCore 0:
  129.0 71.1 all-reduce.11
  260.3 38.1 all-gather.8
  389.0 76.8 reduce-scatter.4
  467.8 28.5 all-gather.4
  498.9 78.4 reduce-scatter.2
  578.8 28.5 all-gather.6
  734.5 67.3 all-reduce.13
  806.1 110.0 all-reduce.15
where the time goes:
time: 941 us; the launch traced here: 927 us
  waiting for transfers between devices  350 us (37%)
  local copies, waits for them, and re-layouts  332 us (35%)
  matrix products  99.7 us (11%)
  other arithmetic  64.3 us (7%)
  blocking collectives  43.5 us (5%)
  starting transfers between devices  22.1 us (2%)
  between operations  15.6 us (2%)
    unnamed x146, local copies, waits for them, and re-layouts  98.3 us
    all_to_all x1, waiting for transfers between devices, per_device(): lax.all_to_all(sent_rows, 'expert', split_axis=0, concat_axis=0, tiled=True)  92.4 us
    rev x2, local copies, waits for them, and re-layouts, gather_diagonals(): flipped = jnp.pad(grid[:, :, ::-1], ((0, 0), (0, 0), (0, row_count)))  63 us
    reduce_scatter x1, waiting for transfers between devices, per_device(): lax.psum_scatter(expert_part, 'tensor', scatter_dimension=3, tiled=True)  57.5 us
    reduce_scatter x1, waiting for transfers between devices, per_device(): lax.psum_scatter(row_part, 'tensor', scatter_dimension=3, tiled=True)  51.5 us
    psum x1, waiting for transfers between devices, per_device(): attn_total = lax.psum(attn_part, 'tensor')  50.5 us
    psum x1, waiting for transfers between devices, per_device(): lax.psum((grad_gain_attn, grad_gain_ffn, grad_weight_qkv, grad_weight_att...  44 us
    psum x1, blocking collectives, per_device(): lax.psum((grad_gain_attn, grad_gain_ffn, grad_weight_qkv, grad_weight_att...  37.4 us
  transfers between devices with their start and end apart: 12, of which 8 were waited for; matrix products, arithmetic and copies ran while one was open for 25% of the time, Pallas kernels for 0%

commit v1 on v0

--- a/solution.py
+++ b/solution.py
@@ -1,8 +1,11 @@
+import functools
 import math
 
 import jax
 import jax.numpy as jnp
 from jax import lax
+from jax.experimental import pallas as pl
+from jax.experimental.pallas import tpu as pltpu
 from jax.sharding import PartitionSpec as P
 
 BLOCK = 512
@@ -12,6 +15,767 @@
 epsilon = 1e-06
 negative = -1e30
 highest = lax.Precision.HIGHEST
+
+
+F32 = jnp.float32
+BF16 = jnp.bfloat16
+MESH = pl.DeviceIdType.MESH
+VMEM_SPEC = pl.BlockSpec(memory_space=pltpu.VMEM)
+ANY_SPEC = pl.BlockSpec(memory_space=pl.ANY)
+LANES = 128
+ROW_TILE = 256
+COL_TILE = 256
+VMEM_LIMIT = 60 * 2**20
+
+
+def dot_nn(left, right):
+    return lax.dot_general(left, right, (((1,), (0,)), ((), ())), preferred_element_type=F32)
+
+
+def dot_nt(left, right):
+    return lax.dot_general(left, right, (((1,), (1,)), ((), ())), preferred_element_type=F32)
+
+
+def dot_tn(left, right):
+    return lax.dot_general(left, right, (((0,), (0,)), ((), ())), preferred_element_type=F32)
+
+
+def round_up(value, step):
+    return (value + step - 1) // step * step
+
+
+class Sizes:
+    def __init__(self, experts, seq_len, top_count, width):
+        self.experts = experts
+        self.seq = seq_len
+        self.width = width
+        self.half_width = width // 2
+        capacity = (4 * seq_len * top_count + 24 * experts - 1) // (24 * experts) * 8
+        self.slots = round_up(capacity, 32)
+        self.half = self.slots // 2
+        self.slot_lanes = round_up(self.slots, LANES)
+
+
+class Place:
+    def __init__(self, sizes):
+        self.count = sizes.experts
+        self.e = lax.axis_index("expert")
+        self.t = lax.axis_index("tensor")
+        self.c = lax.rem(self.t, 2)
+        self.x = lax.div(self.t, 2)
+        self.core_peer = self.t + 1 - 2 * self.c
+        self.x_peer = lax.rem(self.t + 2, 4)
+
+    def ahead(self, k):
+        return lax.rem(self.e + k, self.count)
+
+    def behind(self, k):
+        return lax.rem(self.e + self.count - k, self.count)
+
+    def greet(self, expert_peers=True, all_tensor=True):
+        barrier = pltpu.get_barrier_semaphore()
+        count = 0
+        if expert_peers:
+
+            def one(k, carry):
+                pl.semaphore_signal(
+                    barrier, inc=1, device_id=(self.ahead(k), self.t), device_id_type=MESH
+                )
+                return carry
+
+            lax.fori_loop(1, self.count, one, 0)
+            count += self.count - 1
+        for d in range(1, 4):
+            pl.semaphore_signal(
+                barrier,
+                inc=1,
+                device_id=(self.e, lax.rem(self.t + d, 4)),
+                device_id_type=MESH,
+            )
+        count += 3
+        pl.semaphore_wait(barrier, count)
+
+
+def remote(src, dst, send_sem, recv_sem, device):
+    return pltpu.make_async_remote_copy(
+        src_ref=src,
+        dst_ref=dst,
+        send_sem=send_sem,
+        recv_sem=recv_sem,
+        device_id=device,
+        device_id_type=MESH,
+    )
+
+
+class Gather:
+    sem_kinds = 4
+
+    def __init__(self, sizes, place, stage, buf, send, recv):
+        self.z, self.p = sizes, place
+        self.stage, self.buf, self.send, self.recv = stage, buf, send, recv
+
+    def quarter(self, k, c, x):
+        h, w = self.z.half, self.z.half_width
+        return self.buf.at[
+            k, pl.ds(pl.multiple_of(c * h, 16), h), pl.ds(pl.multiple_of(x * w, LANES), w)
+        ]
+
+    def out(self, k):
+        p = self.p
+        return remote(
+            self.stage.at[k],
+            self.quarter(k, p.c, p.x),
+            self.send.at[0, k],
+            self.recv.at[0, k],
+            (p.ahead(k), p.t),
+        )
+
+    def to_core(self, k):
+        p = self.p
+        ref = self.quarter(k, p.c, p.x)
+        return remote(ref, ref, self.send.at[1, k], self.recv.at[1, k], (p.e, p.core_peer))
+
+    def to_x(self, k):
+        p = self.p
+        ref = self.quarter(k, p.c, p.x)
+        return remote(ref, ref, self.send.at[2, k], self.recv.at[2, k], (p.e, p.x_peer))
+
+    def on_to_core(self, k):
+        p = self.p
+        ref = self.quarter(k, p.c, 1 - p.x)
+        return remote(ref, ref, self.send.at[3, k], self.recv.at[3, k], (p.e, p.core_peer))
+
+    def pack_own(self, rk_row, rows_ref):
+        z, p = self.z, self.p
+        pick = slot_onehot(rk_row[pl.ds(p.e, 1), :], z.slots, 0)
+        for j in range(0, z.width, COL_TILE):
+            self.buf[0, :, j : j + COL_TILE] = dot_nn(
+                pick, rows_ref[:, j : j + COL_TILE]
+            ).astype(BF16)
+
+    def pack(self, k, pick, rows_ref):
+        z, p = self.z, self.p
+        cols = rows_ref[:, pl.ds(pl.multiple_of(p.x * z.half_width, LANES), z.half_width)]
+        self.stage[k] = dot_nn(pick, cols).astype(BF16)
+
+    def first(self, k):
+        self.out(k).wait_recv()
+        self.to_core(k).start()
+        self.to_x(k).start()
+
+    def second(self, k):
+        self.to_x(k).wait_recv()
+        self.on_to_core(k).start()
+
+    def last(self, k):
+        self.to_core(k).wait_recv()
+        self.on_to_core(k).wait_recv()
+
+    def finish(self, k):
+        self.out(k).wait_send()
+        self.to_core(k).wait_send()
+        self.to_x(k).wait_send()
+        self.on_to_core(k).wait_send()
+
+
+class Return:
+    sem_kinds = 3
+
+    def __init__(self, sizes, place, part, from_core, stage_x, from_x, ret, send, recv):
+        self.z, self.p = sizes, place
+        self.part, self.from_core, self.stage_x = part, from_core, stage_x
+        self.from_x, self.ret = from_x, ret
+        self.send, self.recv = send, recv
+
+    def rows(self, c):
+        return pl.ds(pl.multiple_of(c * self.z.half, 16), self.z.half)
+
+    def cols(self, x):
+        return pl.ds(pl.multiple_of(x * self.z.half_width, LANES), self.z.half_width)
+
+    def to_core(self, k):
+        p = self.p
+        return remote(
+            self.part.at[k, self.rows(1 - p.c), :],
+            self.from_core.at[k],
+            self.send.at[0, k],
+            self.recv.at[0, k],
+            (p.e, p.core_peer),
+        )
+
+    def to_x(self, k):
+        p = self.p
+        return remote(
+            self.stage_x.at[k],
+            self.from_x.at[k],
+            self.send.at[1, k],
+            self.recv.at[1, k],
+            (p.e, p.x_peer),
+        )
+
+    def home(self, k):
+        p = self.p
+        return remote(
+            self.from_core.at[k, :, self.cols(p.x)],
+            self.ret.at[k],
+            self.send.at[2, k],
+            self.recv.at[2, k],
+            (p.behind(k), p.t),
+        )
+
+    def first(self, k):
+        self.to_core(k).start()
+
+    def second(self, k):
+        p = self.p
+        self.to_core(k).wait_recv()
+        rows = self.rows(p.c)
+        for x in (1 - p.x, p.x):
+            cols = self.cols(x)
+            both = self.part[k, rows, cols].astype(F32) + self.from_core[k, :, cols].astype(F32)
+            if x is p.x:
+                self.from_core[k, :, cols] = both.astype(BF16)
+            else:
+                self.stage_x[k] = both.astype(BF16)
+                self.to_x(k).start()
+
+    def third(self, k):
+        self.to_x(k).wait_recv()
+        cols = self.cols(self.p.x)
+        total = self.from_core[k, :, cols].astype(F32) + self.from_x[k].astype(F32)
+
+        @pl.when(k == 0)
+        def _():
+            self.ret[0] = total.astype(BF16)
+
+        @pl.when(k > 0)
+        def _():
+            self.from_core[k, :, cols] = total.astype(BF16)
+            self.home(k).start()
+
+    def arrive(self, k):
+        @pl.when(k > 0)
+        def _():
+            self.home(k).wait_recv()
+
+    def finish(self, k):
+        self.to_core(k).wait_send()
+        self.to_x(k).wait_send()
+
+        @pl.when(k > 0)
+        def _():
+            self.home(k).wait_send()
+
+
+def return_scratch(z):
+    e, h, w = z.experts, z.half, z.half_width
+    return [
+        pltpu.VMEM((e, z.slots, z.width), BF16),
+        pltpu.VMEM((e, h, z.width), BF16),
+        pltpu.VMEM((e, h, w), BF16),
+        pltpu.VMEM((e, h, w), BF16),
+        pltpu.VMEM((e, h, w), BF16),
+        pltpu.SemaphoreType.DMA((Return.sem_kinds, e)),
+        pltpu.SemaphoreType.DMA((Return.sem_kinds, e)),
+    ]
+
+
+def gather_scratch(z):
+    e, h, w = z.experts, z.half, z.half_width
+    return [
+        pltpu.VMEM((e, h, w), BF16),
+        pltpu.VMEM((e, z.slots, z.width), BF16),
+        pltpu.SemaphoreType.DMA((Gather.sem_kinds, e)),
+        pltpu.SemaphoreType.DMA((Gather.sem_kinds, e)),
+    ]
+
+
+def slot_onehot(rank_row, count, offset):
+    slot = lax.broadcasted_iota(jnp.int32, (count, rank_row.shape[1]), 0).astype(F32)
+    shift = lax.convert_element_type(offset, F32)
+    return jnp.where(rank_row - shift == slot, 1.0, 0.0).astype(BF16)
+
+
+def pick_lane(values, lane):
+    lanes = lax.broadcasted_iota(jnp.int32, values.shape, 1)
+    return jnp.sum(jnp.where(lanes == lane, values, 0.0), axis=1, keepdims=True)
+
+
+def row_to_col(row, count, offset):
+    rows = lax.broadcasted_iota(jnp.int32, (count, row.shape[1]), 0) + offset
+    lanes = lax.broadcasted_iota(jnp.int32, (count, row.shape[1]), 1)
+    return jnp.sum(jnp.where(rows == lanes, row, 0.0), axis=1, keepdims=True)
+
+
+def col_to_row(col, lane_count):
+    rows = lax.broadcasted_iota(jnp.int32, (col.shape[0], lane_count), 0)
+    lanes = lax.broadcasted_iota(jnp.int32, (col.shape[0], lane_count), 1)
+    return jnp.sum(jnp.where(rows == lanes, col, 0.0), axis=0, keepdims=True)
+
+
+def loop(start, stop, body):
+    def step(i, carry):
+        body(i)
+        return carry
+
+    lax.fori_loop(start, stop, step, 0)
+
+
+def fill_ranks(routes_ref, rk_col, rk_row):
+    seq = routes_ref.shape[0]
+    ids = lax.broadcasted_iota(jnp.int32, (seq, LANES), 1)
+    routes = routes_ref[...]
+    hot = (routes[:, 0:1] == ids) | (routes[:, 1:2] == ids)
+    hot_low = jnp.where(hot, 1.0, 0.0).astype(BF16)
+    hot_mark = jnp.where(hot, 1.0, 0.0)
+    for r in range(0, seq, ROW_TILE):
+        rows = lax.broadcasted_iota(jnp.int32, (ROW_TILE, seq), 0) + r
+        cols = lax.broadcasted_iota(jnp.int32, (ROW_TILE, seq), 1)
+        before = jnp.where(cols < rows, 1.0, 0.0).astype(BF16)
+        rank = dot_nn(before, hot_low)
+        rank = jnp.where(hot_mark[r : r + ROW_TILE] > 0.5, rank, -1.0)
+        rk_col[r : r + ROW_TILE, :] = rank
+        rk_row[:, r : r + ROW_TILE] = rank.T
+
+
+def send_grads_kernel(
+    z, routes_ref, cot_ref, w_out_ref, rk_col, rk_row, og_out, hg_out,
+    stage, buf, g_send, g_recv, hg, out_sem,
+):
+    p = Place(z)
+    fill_ranks(routes_ref, rk_col, rk_row)
+    p.greet()
+    g = Gather(z, p, stage, buf, g_send, g_recv)
+
+    def pack(k):
+        pick = slot_onehot(rk_row[pl.ds(p.ahead(k), 1), :], z.half, p.c * z.half)
+        g.pack(k, pick, cot_ref)
+        g.out(k).start()
+
+    loop(1, z.experts, pack)
+    g.pack_own(rk_row, cot_ref)
+
+    def save(k):
+        return (
+            pltpu.make_async_copy(buf.at[k], og_out.at[k], out_sem.at[0, k]),
+            pltpu.make_async_copy(hg.at[k], hg_out.at[k], out_sem.at[1, k]),
+        )
+
+    def body(i):
+        @pl.when(i + 1 < z.experts)
+        def _():
+            g.first(i + 1)
+
+        @pl.when((i >= 1) & (i < z.experts))
+        def _():
+            g.second(i)
+
+        @pl.when(i >= 2)
+        def _():
+            g.last(i - 1)
+
+        @pl.when(i >= 1)
+        def _():
+            k = i - 1
+            for j in range(0, w_out_ref.shape[0], COL_TILE):
+                hg[k, :, j : j + COL_TILE] = dot_nt(
+                    buf[k], w_out_ref[j : j + COL_TILE, :]
+                ).astype(BF16)
+            for copy in save(k):
+                copy.start()
+
+    loop(0, z.experts + 1, body)
+
+    def finish(k):
+        @pl.when(k > 0)
+        def _():
+            g.finish(k)
+
+        for copy in save(k):
+            copy.wait()
+
+    loop(0, z.experts, finish)
+
+
+def send_grads(z, routes, cot_full, w_out):
+    e = z.experts
+    return pl.pallas_call(
+        functools.partial(send_grads_kernel, z),
+        out_shape=(
+            jax.ShapeDtypeStruct((z.seq, LANES), F32),
+            jax.ShapeDtypeStruct((LANES, z.seq), F32),
+            jax.ShapeDtypeStruct((e, z.slots, z.width), BF16),
+            jax.ShapeDtypeStruct((e, z.slots, w_out.shape[0]), BF16),
+        ),
+        in_specs=[VMEM_SPEC] * 3,
+        out_specs=(VMEM_SPEC, VMEM_SPEC, ANY_SPEC, ANY_SPEC),
+        scratch_shapes=gather_scratch(z)
+        + [
+            pltpu.VMEM((e, z.slots, w_out.shape[0]), BF16),
+            pltpu.SemaphoreType.DMA((2, e)),
+        ],
+        compiler_params=pltpu.CompilerParams(
+            collective_id=1, has_side_effects=True, vmem_limit_bytes=VMEM_LIMIT
+        ),
+        name="send_grads",
+    )(routes, cot_full, w_out)
+
+
+def gelu_pair(h):
+    scale = 0.7978845608028654
+    square = h * h
+    t = jnp.tanh(scale * h * (1.0 + 0.044715 * square))
+    half = 0.5 + 0.5 * t
+    slope = half + (0.5 * scale) * h * (1.0 - t * t) * (1.0 + 0.134145 * square)
+    return h * half, slope
+
+
+def experts_kernel(
+    z, x_ref, mixed_ref, wao_ref, gain_ref, wr_ref, rk_col, rk_row, w_in_ref, hg_ref,
+    mid_ref, nrm_ref, gates_ref, nf_out, gg_out, gs_in, rows_out, hid_out, pre_out,
+    stage, buf, g_send, g_recv,
+    part, from_core, stage_x, from_x, ret, r_send, r_recv,
+    hid, pre, wr_pad, gate_row, gs_out, gg_send, gg_recv, acc, retx,
+    d_send, d_recv, gd_send, gd_recv, nf,
+    gs_sems, gg_sems, out_sem, d_sems,
+):
+    p = Place(z)
+    experts = z.experts
+    wr_pad[...] = jnp.zeros_like(wr_pad)
+    wr_pad[:, 0:experts] = wr_ref[...]
+    for r in range(0, z.seq, ROW_TILE):
+        rows = slice(r, r + ROW_TILE)
+        mid = x_ref[rows, :].astype(F32) + dot_nn(mixed_ref[rows, :], wao_ref[...])
+        mid_ref[rows, :] = mid
+        root = lax.rsqrt(jnp.mean(mid * mid, axis=1, keepdims=True) + epsilon)
+        nrm = (mid * root * gain_ref[...]).astype(BF16)
+        nrm_ref[rows, :] = nrm
+        logits = dot_nn(nrm, wr_pad[...])
+        hot = rk_col[rows, :] > -0.5
+        logits = jnp.where(hot, logits, negative)
+        peak = jnp.max(logits, axis=1, keepdims=True)
+        power = jnp.where(hot, jnp.exp(logits - peak), 0.0)
+        gates = power / jnp.sum(power, axis=1, keepdims=True)
+        gates_ref[rows, :] = gates
+        gate_row[:, rows] = gates.T
+    p.greet()
+    g = Gather(z, p, stage, buf, g_send, g_recv)
+    b = Return(z, p, part, from_core, stage_x, from_x, ret, r_send, r_recv)
+
+    def gate_copy(k):
+        return remote(
+            gs_out.at[k], gs_in.at[k], gs_sems.at[0, k], gs_sems.at[1, k], (p.ahead(k), p.t)
+        )
+
+    def slot_gates(k):
+        pick = slot_onehot(rk_row[pl.ds(p.ahead(k), 1), :], z.slot_lanes, 0)
+        row = gate_row[pl.ds(p.ahead(k), 1), :]
+        high = row.astype(BF16).astype(F32)
+        low = row - high
+        which = lax.broadcasted_iota(jnp.int32, (16, z.seq), 0)
+        both = jnp.where(which == 0, high, jnp.where(which == 1, low, 0.0)).astype(BF16)
+        sums = dot_nt(both, pick)
+        return sums[0:1, :] + sums[1:2, :]
+
+    def pack(k):
+        pick = slot_onehot(rk_row[pl.ds(p.ahead(k), 1), :], z.half, p.c * z.half)
+        g.pack(k, pick, nrm_ref)
+        g.out(k).start()
+
+    loop(1, experts, pack)
+
+    def send_gates(k):
+        gs_out[k] = slot_gates(k)
+        gate_copy(k).start()
+
+    loop(1, experts, send_gates)
+    gs_in[0] = slot_gates(0)
+    g.pack_own(rk_row, nrm_ref)
+
+    def gg_copy(k, d):
+        return remote(
+            gg_send.at[k],
+            gg_recv.at[k, p.t],
+            gg_sems.at[0, k, d],
+            gg_sems.at[1, k, d],
+            (p.behind(k), lax.rem(p.t + d, 4)),
+        )
+
+    def save(k):
+        return (
+            pltpu.make_async_copy(buf.at[k], rows_out.at[k], out_sem.at[0, k]),
+            pltpu.make_async_copy(hid.at[k], hid_out.at[k], out_sem.at[1, k]),
+            pltpu.make_async_copy(pre.at[k], pre_out.at[k], out_sem.at[2, k]),
+        )
+
+    def expert(k):
+        @pl.when(k > 0)
+        def _():
+            gate_copy(k).wait_recv()
+            g.last(k)
+
+        gate = row_to_col(gs_in[k], z.slots, 0)
+        sums = jnp.zeros((z.slots, 1), F32)
+        for j in range(0, w_in_ref.shape[1], COL_TILE):
+            cols = slice(j, j + COL_TILE)
+            up, slope = gelu_pair(dot_nn(buf[k], w_in_ref[:, cols]))
+            back = hg_ref[k, :, cols].astype(F32)
+            hid[k, :, cols] = up.astype(BF16)
+            pre[k, :, cols] = (gate * back * slope).astype(BF16)
+            sums = sums + jnp.sum(up * back, axis=1, keepdims=True)
+        for j in range(0, z.width, COL_TILE):
+            part[k, :, j : j + COL_TILE] = dot_nt(
+                pre[k], w_in_ref[j : j + COL_TILE, :]
+            ).astype(BF16)
+        b.first(k)
+        gg_send[k] = col_to_row(sums, z.slot_lanes)
+        for d in range(1, 4):
+            gg_copy(k, d).start()
+
+        @pl.when(k > 0)
+        def _():
+            gg_copy(k, 0).start()
+
+        @pl.when(k == 0)
+        def _():
+            gg_recv[0, p.t] = gg_send[0]
+
+        for copy in save(k):
+            copy.start()
+
+    def body(i):
+        @pl.when(i < experts)
+        def _():
+            expert(i)
+
+        @pl.when(i == 0)
+        def _():
+            g.first(1)
+
+        @pl.when(i + 2 < experts)
+        def _():
+            g.first(i + 2)
+
+        @pl.when(i + 1 < experts)
+        def _():
+            g.second(i + 1)
+
+        @pl.when((i >= 1) & (i <= experts))
+        def _():
+            b.second(i - 1)
+
+        @pl.when(i >= 2)
+        def _():
+            b.third(i - 2)
+
+    loop(0, experts + 2, body)
+    acc[...] = jnp.zeros_like(acc)
+
+    def combine(k):
+        b.arrive(k)
+        for d in range(1, 4):
+            gg_copy(k, d).wait_recv()
+
+        @pl.when(k > 0)
+        def _():
+            gg_copy(k, 0).wait_recv()
+
+        row = gg_recv[k, 0] + gg_recv[k, 1] + gg_recv[k, 2] + gg_recv[k, 3]
+        col = row_to_col(row, z.half, p.c * z.half)
+        high = col.astype(BF16).astype(F32)
+        lanes = lax.broadcasted_iota(jnp.int32, (z.half, LANES), 1)
+        who = p.ahead(k)
+        retx[:, 0 : z.half_width] = ret[k]
+        retx[:, z.half_width :] = jnp.where(
+            lanes == who, high, jnp.where(lanes == who + experts, col - high, 0.0)
+        ).astype(BF16)
+        for r in range(0, z.seq, ROW_TILE):
+            rows = slice(r, r + ROW_TILE)
+            rank = pick_lane(rk_col[rows, :], who) - lax.convert_element_type(p.c * z.half, F32)
+            slot = lax.broadcasted_iota(jnp.int32, (ROW_TILE, z.half), 1).astype(F32)
+            pick = jnp.where(rank == slot, 1.0, 0.0).astype(BF16)
+            acc[rows, :] += dot_nn(pick, retx[...])
+
+    loop(0, experts, combine)
+    half_seq = z.seq // 2
+
+    def tokens(c):
+        return pl.ds(pl.multiple_of(c * half_seq, 16), half_seq)
+
+    d_send[...] = acc[tokens(1 - p.c), 0 : z.half_width].astype(BF16)
+    gd_send[...] = acc[:, z.half_width :].astype(BF16)
+    copy_d = remote(d_send, d_recv, d_sems.at[0, 0], d_sems.at[1, 0], (p.e, p.core_peer))
+    copy_g = remote(gd_send, gd_recv, d_sems.at[0, 1], d_sems.at[1, 1], (p.e, p.core_peer))
+    copy_d.start()
+    copy_g.start()
+    copy_d.wait_recv()
+
+    def piece(x):
+        return nf.at[tokens(p.c), pl.ds(pl.multiple_of(x * z.half_width, LANES), z.half_width)]
+
+    piece(p.x)[...] = (
+        acc[tokens(p.c), 0 : z.half_width] + d_recv[...].astype(F32)
+    ).astype(BF16)
+    to_x = remote(piece(p.x), piece(p.x), d_sems.at[0, 2], d_sems.at[1, 2], (p.e, p.x_peer))
+    to_core = remote(piece(p.x), piece(p.x), d_sems.at[0, 3], d_sems.at[1, 3], (p.e, p.core_peer))
+    on_to_core = remote(
+        piece(1 - p.x), piece(1 - p.x), d_sems.at[0, 4], d_sems.at[1, 4], (p.e, p.core_peer)
+    )
+    to_x.start()
+    to_core.start()
+    copy_g.wait_recv()
+    gg_out[...] = acc[:, z.half_width :] + gd_recv[...].astype(F32)
+
+    def finish(k):
+        b.finish(k)
+        for d in range(1, 4):
+            gg_copy(k, d).wait_send()
+
+        @pl.when(k > 0)
+        def _():
+            g.finish(k)
+            gate_copy(k).wait_send()
+            gg_copy(k, 0).wait_send()
+
+        for copy in save(k):
+            copy.wait()
+
+    loop(0, experts, finish)
+    to_x.wait_recv()
+    on_to_core.start()
+    to_core.wait_recv()
+    on_to_core.wait_recv()
+    nf_out[...] = nf[...]
+    for copy in (copy_d, copy_g, to_x, to_core, on_to_core):
+        copy.wait_send()
+
+
+def run_experts(z, inputs, mixed_all, wao_full, gain_ffn, weight_router, rk_col, rk_row, w_in, hg):
+    e = z.experts
+    hidden_count = w_in.shape[1]
+    rows_shape = jax.ShapeDtypeStruct((e, z.slots, z.width), BF16)
+    hid_shape = jax.ShapeDtypeStruct((e, z.slots, hidden_count), BF16)
+    half_seq = z.seq // 2
+    return pl.pallas_call(
+        functools.partial(experts_kernel, z),
+        out_shape=(
+            jax.ShapeDtypeStruct((z.seq, z.width), F32),
+            jax.ShapeDtypeStruct((z.seq, z.width), BF16),
+            jax.ShapeDtypeStruct((z.seq, LANES), F32),
+            jax.ShapeDtypeStruct((z.seq, z.width), BF16),
+            jax.ShapeDtypeStruct((z.seq, LANES), F32),
+            jax.ShapeDtypeStruct((e, 1, z.slot_lanes), F32),
+            rows_shape,
+            hid_shape,
+            hid_shape,
+        ),
+        in_specs=[VMEM_SPEC] * 9,
+        out_specs=(VMEM_SPEC,) * 6 + (ANY_SPEC,) * 3,
+        scratch_shapes=gather_scratch(z)
+        + return_scratch(z)
+        + [
+            pltpu.VMEM((e, z.slots, hidden_count), BF16),
+            pltpu.VMEM((e, z.slots, hidden_count), BF16),
+            pltpu.VMEM((z.width, LANES), BF16),
+            pltpu.VMEM((LANES, z.seq), F32),
+            pltpu.VMEM((e, 1, z.slot_lanes), F32),
+            pltpu.VMEM((e, 1, z.slot_lanes), F32),
+            pltpu.VMEM((e, 4, 1, z.slot_lanes), F32),
+            pltpu.VMEM((z.seq, z.half_width + LANES), F32),
+            pltpu.VMEM((z.half, z.half_width + LANES), BF16),
+            pltpu.VMEM((half_seq, z.half_width), BF16),
+            pltpu.VMEM((half_seq, z.half_width), BF16),
+            pltpu.VMEM((z.seq, LANES), BF16),
+            pltpu.VMEM((z.seq, LANES), BF16),
+            pltpu.VMEM((z.seq, z.width), BF16),
+            pltpu.SemaphoreType.DMA((2, e)),
+            pltpu.SemaphoreType.DMA((2, e, 4)),
+            pltpu.SemaphoreType.DMA((3, e)),
+            pltpu.SemaphoreType.DMA((2, 5)),
+        ],
+        compiler_params=pltpu.CompilerParams(
+            collective_id=2, has_side_effects=True, vmem_limit_bytes=VMEM_LIMIT
+        ),
+        name="run_experts",
+    )(
+        inputs, mixed_all, wao_full, gain_ffn.reshape(1, -1), weight_router, rk_col, rk_row,
+        w_in, hg,
+    )
+
+
+def results_kernel(
+    z, hid_ref, w_out_ref, rk_col, gates_ref, mid_ref, out_ref,
+    part, from_core, stage_x, from_x, ret, r_send, r_recv,
+    acc, d_send, d_recv, d_sems,
+):
+    p = Place(z)
+    p.greet()
+    b = Return(z, p, part, from_core, stage_x, from_x, ret, r_send, r_recv)
+
+    def body(i):
+        @pl.when(i < z.experts)
+        def _():
+            for j in range(0, z.width, COL_TILE):
+                part[i, :, j : j + COL_TILE] = dot_nn(
+                    hid_ref[i], w_out_ref[:, j : j + COL_TILE]
+                ).astype(BF16)
+            b.first(i)
+
+        @pl.when((i >= 1) & (i <= z.experts))
+        def _():
+            b.second(i - 1)
+
+        @pl.when(i >= 2)
+        def _():
+            b.third(i - 2)
+
+    loop(0, z.experts + 2, body)
+    acc[...] = jnp.zeros_like(acc)
+
+    def combine(k):
+        b.arrive(k)
+        who = p.ahead(k)
+        for r in range(0, z.seq, ROW_TILE):
+            rows = slice(r, r + ROW_TILE)
+            rank = pick_lane(rk_col[rows, :], who) - lax.convert_element_type(p.c * z.half, F32)
+            slot = lax.broadcasted_iota(jnp.int32, (ROW_TILE, z.half), 1).astype(F32)
+            pick = jnp.where(rank == slot, 1.0, 0.0).astype(BF16)
+            acc[rows, :] += pick_lane(gates_ref[rows, :], who) * dot_nn(pick, ret[k])
+
+    loop(0, z.experts, combine)
+    own = z.half_width // 2
+    first = acc[:, 0:own]
+    second = acc[:, own:]
+    d_send[...] = jnp.where(p.c == 0, second, first).astype(BF16)
+    copy = remote(d_send, d_recv, d_sems.at[0], d_sems.at[1], (p.e, p.core_peer))
+    copy.start()
+    mid = mid_ref[:, pl.ds(pl.multiple_of(p.x * z.half_width, LANES), z.half_width)]
+    mine = jnp.where(p.c == 0, first + mid[:, 0:own], second + mid[:, own:])
+    copy.wait_recv()
+    out_ref[...] = (mine + d_recv[...].astype(F32)).astype(BF16)
+    copy.wait_send()
+    loop(0, z.experts, b.finish)
+
+
+def return_results(z, hid, w_out, rk_col, gates, mid):
+    own = z.half_width // 2
+    return pl.pallas_call(
+        functools.partial(results_kernel, z),
+        out_shape=jax.ShapeDtypeStruct((z.seq, own), BF16),
+        in_specs=[VMEM_SPEC] * 5,
+        out_specs=VMEM_SPEC,
+        scratch_shapes=return_scratch(z)
+        + [
+            pltpu.VMEM((z.seq, z.half_width), F32),
+            pltpu.VMEM((z.seq, own), BF16),
+            pltpu.VMEM((z.seq, own), BF16),
+            pltpu.SemaphoreType.DMA((2,)),
+        ],
+        compiler_params=pltpu.CompilerParams(
+            collective_id=3, has_side_effects=True, vmem_limit_bytes=VMEM_LIMIT
+        ),
+        name="return_results",
+    )(hid, w_out, rk_col, gates, mid)
 
 
 def far_limits(buckets):
@@ -104,12 +868,7 @@
     block_rows = min(BLOCK, seq_len)
     block_count = seq_len // block_rows
     experts = weight_router.shape[1]
-    local_experts = weight_in.shape[0]
-    source_count = experts // local_experts
     top_count = routes.shape[1]
-    capacity = (4 * seq_len * top_count + 24 * experts - 1) // (24 * experts) * 8
-    out_width = cotangent.shape[1]
-    column_start = lax.axis_index("tensor") * out_width
     stream_in = inputs.astype(jnp.float32)
     root_attn = lax.rsqrt(jnp.mean(stream_in * stream_in, axis=-1, keepdims=True) + epsilon)
     unit_attn = stream_in * root_attn
@@ -148,132 +907,39 @@
     mixed_heads = (
         jnp.concatenate(mixed_parts, axis=0).reshape(seq_len, col_width).astype(jnp.bfloat16)
     )
-    attn_part = jnp.dot(mixed_heads, weight_attn_out, preferred_element_type=jnp.float32)
-    attn_total = lax.psum(attn_part, "tensor")
-    stream_mid = stream_in + attn_total
+    z = Sizes(experts, seq_len, top_count, width)
+    cot_full = lax.all_gather(cotangent, "tensor", axis=1, tiled=True)
+    rk_col, rk_row, og_rows, hg = send_grads(z, routes, cot_full, weight_out[0])
+    mixed_all = lax.all_gather(mixed_heads, "tensor", axis=1, tiled=True)
+    wao_full = lax.all_gather(weight_attn_out, "tensor", axis=0, tiled=True)
+    stream_mid, normed_ffn, gates, normed_part, gate_pairs, gate_slots, slot_rows, hidden, pre_grads = run_experts(
+        z, inputs, mixed_all, wao_full, gain_ffn, weight_router, rk_col, rk_row, weight_in[0], hg
+    )
+    activations = return_results(z, hidden, weight_out[0], rk_col, gates, stream_mid)
+    flat = (experts * z.slots, -1)
+    grad_weight_in = jnp.einsum(
+        "sd,sf->df", slot_rows.reshape(flat), pre_grads.reshape(flat), preferred_element_type=jnp.float32
+    )[None]
+    slot_grads = (gate_slots[:, 0, : z.slots, None] * og_rows.astype(jnp.float32)).astype(jnp.bfloat16)
+    grad_weight_out = jnp.einsum(
+        "sf,sd->fd", hidden.reshape(flat), slot_grads.reshape(flat), preferred_element_type=jnp.float32
+    )[None]
     root_ffn = lax.rsqrt(jnp.mean(stream_mid * stream_mid, axis=-1, keepdims=True) + epsilon)
     unit_ffn = stream_mid * root_ffn
-    normed_ffn = (unit_ffn * gain_ffn).astype(jnp.bfloat16)
-    logits = jnp.dot(normed_ffn, weight_router, preferred_element_type=jnp.float32)
-    expert_ids = jnp.arange(experts, dtype=jnp.int32)
-    route_hot = routes[:, :, None] == expert_ids[None, None, :]
-    chosen = jnp.sum(jnp.where(route_hot, logits[:, None, :], 0.0), axis=-1)
-    gate_weights = jax.nn.softmax(chosen, axis=-1)
-    route_flat = routes.reshape(-1)
-    route_count = route_flat.shape[0]
-    flat_hot = (route_flat[:, None] == expert_ids[None, :]).astype(jnp.int32)
-    earlier = jnp.cumsum(flat_hot, axis=0) - flat_hot
-    slot_rank = jnp.sum(earlier * flat_hot, axis=1)
-    slot_index = route_flat * capacity + slot_rank
-    slot_route = (
-        jnp.full((experts * capacity,), route_count, jnp.int32)
-        .at[slot_index]
-        .set(jnp.arange(route_count, dtype=jnp.int32))
-    )
-    slot_token = jnp.where(slot_route < route_count, slot_route // top_count, seq_len)
-    padded_rows = jnp.concatenate([normed_ffn, jnp.zeros((1, width), jnp.bfloat16)], axis=0)
-    sent_rows = padded_rows[slot_token].reshape(experts, capacity, width)
-    arrived = lax.all_to_all(sent_rows, "expert", split_axis=0, concat_axis=0, tiled=True)
-    arrived = arrived.reshape(source_count, local_experts, capacity, width)
-    hidden_pre = jnp.einsum(
-        "nlcd,ldf->nlcf", arrived, weight_in, preferred_element_type=jnp.float32
-    )
-    hidden = jax.nn.gelu(hidden_pre).astype(jnp.bfloat16)
-    expert_part = jnp.einsum(
-        "nlcf,lfd->nlcd", hidden, weight_out, preferred_element_type=jnp.float32
-    )
-    expert_share = lax.psum_scatter(expert_part, "tensor", scatter_dimension=3, tiled=True).astype(
-        jnp.bfloat16
-    )
-    returned = lax.all_to_all(
-        expert_share.reshape(experts, capacity, out_width),
-        "expert",
-        split_axis=0,
-        concat_axis=0,
-        tiled=True,
-    )
-    picked = (
-        returned.reshape(experts * capacity, out_width)[slot_index]
-        .astype(jnp.float32)
-        .reshape(seq_len, top_count, out_width)
-    )
-    combined = jnp.sum(gate_weights[:, :, None] * picked, axis=1)
-    activations = (
-        lax.dynamic_slice_in_dim(stream_mid, column_start, out_width, 1) + combined
-    ).astype(jnp.bfloat16)
-    out_grad = cotangent.astype(jnp.float32)
-    gate_part = jnp.sum(out_grad[:, None, :] * picked, axis=-1)
-    slot_grads = (
-        (gate_weights[:, :, None] * out_grad[:, None, :])
-        .astype(jnp.bfloat16)
-        .reshape(route_count, out_width)
-    )
-    slot_grads = jnp.concatenate([slot_grads, jnp.zeros((1, out_width), jnp.bfloat16)], axis=0)[
-        slot_route
-    ]
-    result_grads = lax.all_to_all(
-        slot_grads.reshape(experts, capacity, out_width),
-        "expert",
-        split_axis=0,
-        concat_axis=0,
-        tiled=True,
-    )
-    result_grads = lax.all_gather(
-        result_grads.reshape(source_count, local_experts, capacity, out_width),
-        "tensor",
-        axis=3,
-        tiled=True,
-    )
-    hidden_grads = jnp.einsum(
-        "nlcd,lfd->nlcf", result_grads, weight_out, preferred_element_type=jnp.float32
-    )
-    grad_weight_out = jnp.einsum(
-        "nlcf,nlcd->lfd", hidden, result_grads, preferred_element_type=jnp.float32
-    )
-    gelu_back = jax.vjp(jax.nn.gelu, hidden_pre)[1]
-    pre_grads = gelu_back(hidden_grads)[0].astype(jnp.bfloat16)
-    grad_weight_in = jnp.einsum(
-        "nlcd,nlcf->ldf", arrived, pre_grads, preferred_element_type=jnp.float32
-    )
-    row_part = jnp.einsum(
-        "nlcf,ldf->nlcd", pre_grads, weight_in, preferred_element_type=jnp.float32
-    )
-    row_share = lax.psum_scatter(row_part, "tensor", scatter_dimension=3, tiled=True).astype(
-        jnp.bfloat16
-    )
-    row_back = lax.all_to_all(
-        row_share.reshape(experts, capacity, out_width),
-        "expert",
-        split_axis=0,
-        concat_axis=0,
-        tiled=True,
-    )
-    normed_part = jnp.sum(
-        row_back.reshape(experts * capacity, out_width)[slot_index]
-        .astype(jnp.float32)
-        .reshape(seq_len, top_count, out_width),
-        axis=1,
-    )
-    gate_grads = lax.psum(gate_part, "tensor")
-    chosen_grads = gate_weights * (
+    gate_weights = gates[:, :experts]
+    gate_grads = gate_pairs[:, :experts] + gate_pairs[:, experts : 2 * experts]
+    logit_grads = (gate_weights * (
         gate_grads - jnp.sum(gate_weights * gate_grads, axis=-1, keepdims=True)
-    )
-    logit_grads = jnp.sum(jnp.where(route_hot, chosen_grads[:, :, None], 0.0), axis=1).astype(
-        jnp.bfloat16
-    )
+    )).astype(jnp.bfloat16)
     grad_weight_router = jnp.einsum(
         "td,te->de", normed_ffn, logit_grads, preferred_element_type=jnp.float32
     )
     router_back = jnp.einsum(
         "te,de->td", logit_grads, weight_router, preferred_element_type=jnp.float32
     )
-    normed_grads, stream_grads = (
-        lax.all_gather(normed_part, "tensor", axis=1, tiled=True),
-        lax.all_gather(out_grad, "tensor", axis=1, tiled=True),
-    )
-    normed_grads = normed_grads + router_back
+    normed_grads = normed_part.astype(jnp.float32) + router_back
     grad_gain_ffn = jnp.sum(normed_grads * unit_ffn, axis=0)
-    mid_grads = stream_grads + norm_back(normed_grads, unit_ffn, root_ffn, gain_ffn)
+    mid_grads = cot_full.astype(jnp.float32) + norm_back(normed_grads, unit_ffn, root_ffn, gain_ffn)
     attn_grads = mid_grads.astype(jnp.bfloat16)
     grad_weight_attn_out = jnp.einsum(
         "tc,td->cd", mixed_heads, attn_grads, preferred_element_type=jnp.float32

time: 941 us -> 676 us (0.72)
  waiting for transfers between devices: 350 us -> 53.6 us
  Pallas kernels: 0 us -> 218 us
  local copies, waits for them, and re-layouts: 332 us -> 236 us
  matrix products: 99.7 us -> 62.1 us
  starting transfers between devices: 22.1 us -> 0.2 us
  other arithmetic: 64.3 us -> 42.7 us
    pallas_call x0 -> x3, Pallas kernels: none -> 218 us  [the longest x1 103 us: run_experts(): pl.pallas_call(functools.partial(experts_kernel, z), out_shape=(jax.Shape...]
    all_to_all x4 -> x0, waiting for transfers between devices: 145 us -> none  [the longest x1 92.4 us: per_device(): lax.all_to_all(sent_rows, 'expert', split_axis=0, concat_axis=0, tiled=True)]
    reduce_scatter x2 -> x0, waiting for transfers between devices: 109 us -> none  [the longest x1 57.5 us: per_device(): lax.psum_scatter(expert_part, 'tensor', scatter_dimension=3, tiled=True)]
    psum x1 -> x0, waiting for transfers between devices: 50.5 us -> none  [per_device(): attn_total = lax.psum(attn_part, 'tensor')]
    dot_general x8 -> x2, matrix products: 63.8 us -> 17.4 us  [the longest x1 8.85 us: per_device(): jnp.einsum('sf,sd->fd', hidden.reshape(flat), slot_grads.reshape(flat), p...]
    gather x4 -> x0, local copies, waits for them, and re-layouts: 34.7 us -> none  [the longest x1 9.31 us: per_device(): sent_rows = padded_rows[slot_token].reshape(experts, capacity, width)]
    all_to_all x4 -> x0, starting transfers between devices: 21.1 us -> none  [the longest x1 5.54 us: per_device(): lax.all_to_all(row_share.reshape(experts, capacity, out_width), 'expert',...]
    transpose x2 -> x0, local copies, waits for them, and re-layouts: 19.3 us -> none  [the longest x1 9.88 us: per_device(): jnp.einsum('nlcf,lfd->nlcd', hidden, weight_out, preferred_element_type=j...]
  transfers between devices with their start and end apart: 12 -> 5, of which waited for: 8 -> 1; matrix products, arithmetic and copies ran while one was open for 25% -> 30% of each run, Pallas kernels for 0% -> 17%
where the time goes in v1:
time: 676 us; the launch traced here: 663 us
  local copies, waits for them, and re-layouts  236 us (35%)
  Pallas kernels  218 us (32%)
  matrix products  62.1 us (9%)
  waiting for transfers between devices  53.6 us (8%)
  other arithmetic  42.7 us (6%)
  blocking collectives  35.8 us (5%)
  between operations  14.8 us (2%)
    pallas_call x1, Pallas kernels, run_experts(): pl.pallas_call(functools.partial(experts_kernel, z), out_shape=(jax.Shape...  103 us
    unnamed x124, local copies, waits for them, and re-layouts  89.7 us
    rev x2, local copies, waits for them, and re-layouts, gather_diagonals(): flipped = jnp.pad(grid[:, :, ::-1], ((0, 0), (0, 0), (0, row_count)))  62.8 us
    pallas_call x1, Pallas kernels, return_results(): pl.pallas_call(functools.partial(results_kernel, z), out_shape=jax.ShapeD...  62.2 us
    pallas_call x1, Pallas kernels, send_grads(): pl.pallas_call(functools.partial(send_grads_kernel, z), out_shape=(jax.Sh...  52.7 us
    psum x1, waiting for transfers between devices, per_device(): lax.psum((grad_gain_attn, grad_gain_ffn, grad_weight_qkv, grad_weight_att...  52.2 us
    psum x1, blocking collectives, per_device(): lax.psum((grad_gain_attn, grad_gain_ffn, grad_weight_qkv, grad_weight_att...  35.8 us
    reshape x2, local copies, waits for them, and re-layouts, block_bias(): return repeated.reshape(head_count, row_count, wide_count)[:, :, :col_count]  29.1 us
  transfers between devices with their start and end apart: 5, of which 1 were waited for; matrix products, arithmetic and copies ran while one was open for 30% of the time, Pallas kernels for 17%

profile of v1, /device:TPU:0, one launch (start us, length us, event | category | flops | bytes accessed | tf_op | source)
XLA Modules:
  0.0 663.0 jit_solution(4607117675609438626)
XLA Ops:
  24.9 7.1 %copy.75 = f32[1,3,512,1024]{3,1,2,0:T(4,128)S(1)} copy(f32[1,3,512,1024]{3,2,1,0:T(8,128)} %broadcast_bitcast_fusion.1) | data formatting | bytes 12582912
  32.0 4.3 slice.161
  36.3 13.2 %reshape.241 = f32[3,512,1023]{2,1,0:T(8,128)} reshape(f32[3,523776]{1,0:T(4,128)} %slice.161) | data formatting | bytes 12570624 | tf_op jit(solution)/shard_map/reshape | solution.py:814
  58.3 19.9 %copy.76 = f32[1,3,512,1536]{3,1,2,0:T(4,128)S(1)} copy(f32[1,3,512,1536]{3,2,1,0:T(8,128)S(1)} %broadcast_bitcast_fusion) | data formatting | bytes 18874368
  78.1 6.0 slice.168
  84.2 13.2 %reshape.254 = f32[2357760]{0:T(1024)} reshape(f32[3,785920]{1,0:T(4,128)} %slice.168) | data formatting | bytes 18862080
  97.4 15.9 %reshape.242 = f32[3,512,1535]{2,1,0:T(8,128)} reshape(f32[2357760]{0:T(1024)} %reshape.254) | data formatting | bytes 18862080 | tf_op jit(solution)/shard_map/reshape | solution.py:814
  133.5 52.7 %send_grads.1 = (f32[1024,128]{1,0:T(8,128)}, f32[128,1024]{1,0:T(8,128)}, bf16[8,352,768]{2,1,0:T(8,128)(2,1)}, bf16[8,352,768]{2,1,0:T(8,128)(2,1)}) custom-call(s32[1024,2]{1,0:T(8,128)} %copy.58.routes_ref, bf16[1024,768]{1,0:T(8,128)(2,1)} %copy.59.cot_ref, bf16[768,768]{1,0:T(8,128)(2,1)} %bitcast.123), custom_call_target="tpu_custom_call" | custom-call | tf_op jit(solution)/shard_map/send_grads/pallas_call | solution.py:402
  188.8 103.3 %run_experts.1 = (f32[1024,768]{1,0:T(8,128)}, bf16[1024,768]{1,0:T(8,128)(2,1)}, f32[1024,128]{1,0:T(8,128)}, bf16[1024,768]{1,0:T(8,128)(2,1)}, f32[1024,128]{...) custom-call(bf16[1024,768]{1,0:T(8,128)(2,1)} %x_ref.1, ...), custom_call_target="tpu_custom_call" | custom-call | tf_op jit(solution)/shard_map/run_experts/pallas_call | solution.py:659
  307.4 15.3 %rev.26 = bf16[3,512,512]{1,2,0:T(8,128)(2,1)} reverse(bf16[3,512,512]{1,2,0:T(8,128)(2,1)S(1)} %multiply_convert_fusion.3), dimensions={2} | reverse | bytes 3145728 | tf_op jit(solution)/shard_map/rev | solution.py:826
  332.3 47.5 %rev.27 = bf16[3,512,1024]{2,1,0:T(8,128)(2,1)} reverse(bf16[3,512,1024]{2,1,0:T(8,128)(2,1)} %copy-done.4), dimensions={2} | reverse | bytes 6291456 | tf_op jit(solution)/shard_map/rev | solution.py:826
  379.8 4.8 fusion.42
  395.0 13.2 %reshape.246 = f32[3,512,1023]{2,1,0:T(8,128)} reshape(f32[3,523776]{1,0:T(4,128)} %slice_convert_fusion.1) | data formatting | bytes 12570624 | tf_op jit(solution)/shard_map/convert_element_type | solution.py:830
  414.7 6.7 %copy.78 = bf16[1,3,512,1536]{3,1,2,0:T(4,128)(2,1)} copy(bf16[1,3,512,1536]{3,2,1,0:T(8,128)(2,1)S(1)} %pad_bitcast_fusion) | data formatting | bytes 9437184
  424.7 8.7 %slice_convert_fusion = f32[3,785920]{1,0:T(4,128)} fusion(bf16[3,786432]{1,0:T(4,128)(2,1)} %bitcast.121), kind=kLoop, calls=%fused_computation.8 | loop fusion | flops 2357760 | bytes 14146560 | tf_op jit(solution)/shard_map/convert_element_type | solution.py:830
  434.4 62.2 %return_results.1 = bf16[1024,192]{1,0:T(8,128)(2,1)} custom-call(bf16[8,352,768]{2,1,0:T(8,128)(2,1)} %get-tuple-element.26.hid_ref, bf16[768,768]{1,0:T(8,128)(2,1)} %bitcast.124, f32[1024,128]{1,0:T(8,128)} %get-tuple-element.23.rk_col, f32[1024,128]{1,0:T(8,128)} %get-tuple-element.27.gates_ref, f32[1024,768]{1,0:T(8,128)} %get-tuple-element.28.mid_ref), custom_call_target="tpu_custom_call" | custom-call | tf_op jit(solution)/shard_map/return_results/pallas_call | solution.py:762
  498.6 13.2 %reshape.256 = f32[2357760]{0:T(1024)} reshape(f32[3,785920]{1,0:T(4,128)} %slice_convert_fusion) | data formatting | bytes 18862080
  511.8 15.8 %reshape.247 = f32[3,512,1535]{2,1,0:T(8,128)} reshape(f32[2357760]{0:T(1024)} %reshape.256) | data formatting | bytes 18862080 | tf_op jit(solution)/shard_map/convert_element_type | solution.py:830
  527.7 4.4 reduce_sum.149
  537.3 8.5 %convolution_bitcast_fusion.2 = f32[1,768,768]{2,1,0:T(8,128)} fusion(bf16[8,352,768]{2,1,0:T(8,128)(2,1)} %get-tuple-element.32, bf16[8,352,768]{2,1,0:T(8,128)(2,1)} %get-tuple-element.33), kind=kOutput, calls=%fused_computation.52 | convolution fusion | flops 3321888768 | bytes 11010048 | tf_op jit(solution)/shard_map/sd,sf->df/dot_general | solution.py:920
  547.6 8.9 %fusion.23 = f32[1,768,768]{2,1,0:T(8,128)} fusion(bf16[8,352,768]{2,1,0:T(8,128)(2,1)} %get-tuple-element.26.hid_ref, bf16[8,352,768]{2,1,0:T(8,128)(2,1)} %get-tuple-element.35, f32[8,352]{1,0:T(8,128)S(1)} %bitcast.154), kind=kOutput, calls=%fused_computation.51 | convolution fusion | flops 3328376832 | bytes 11021312 | tf_op jit(solution)/shard_map/sf,sd->fd/dot_general | solution.py:924
  559.3 35.8 %all-reduce.4 = (f32[768]{0:T(1024)}, f32[768]{0:T(1024)}, f32[32,3]{0,1:T(4,128)}, f32[768,8]{0,1:T(8,128)}) all-reduce(f32[768]{0:T(1024)S(1)} %get-tuple-element.78, f32[768]{0:T(1024)S(1)} %get-tuple-element.76, f32[32,3]{0,1:T(4,128)S(1)} %copy-done.48, f32[768,8]{0,1:T(8,128)S(1)} %fusion.76), channel_id=1, replica_groups=mesh['expert'=8,'tensor'=4] {'expert'}, use_global_device_ids=true, to_apply=%region_15.16 | all-reduce | flops 7776 | bytes 62208 | tf_op jit(solution)/shard_map/psum | solution.py:1012
  595.1 5.3 fusion.13
  600.5 52.2 %all-reduce.11.cloned.1.call-done = (f32[3,768,192]{1,2,0:T(8,128)}, f32[192,768]{1,0:T(8,128)}) async-done(((f32[3,768,192]{1,2,0:T(8,128)}, f32[192,768]{1,0:T(8,128)}), (f32[3,768,192]{1,2,0:T(8,128)}, f32[192,768]{1,0:T(8,128)})) %all-reduce.11.cloned.1.call-update) | async-done | bytes 2359312 | tf_op jit(solution)/shard_map/psum | solution.py:1012
  (211 shorter events, 110.3 us)
Async XLA Ops:
  7.2 6.6 copy-start
  7.2 123.2 %all-gather.8.cloned.1.call-start = ((), (), s32[]{:S(2)}) async-start(), calls=%async_computation.2 | async-start | bytes 1966080 | tf_op jit(solution)/shard_map/all_gather | solution.py:911
  7.9 178.3 %all-gather.4.cloned.1.call-start = ((), (), s32[]{:S(2)}) async-start(), calls=%async_computation | async-start | bytes 1966080 | tf_op jit(solution)/shard_map/all_gather | solution.py:913
  9.9 6.5 copy-start.36
  97.3 16.0 %slice-start.6 = ((s32[1024]{0:T(1024)}), s32[512]{0:T(512)S(1)}, s32[]{:S(2)}) async-start(s32[1024]{0:T(1024)} %copy-done.37), calls=%async_computation.11 | async-start | bytes 4096 | tf_op jit(solution)/shard_map/slice | solution.py:818
  97.3 16.3 %copy-start.40 = (s32[1024]{0:T(1024)S(1)}, s32[1024]{0:T(1024)}, u32[]{:S(2)}) copy-start(s32[1024]{0:T(1024)} %param.24) | copy-start | bytes 12292
  97.4 16.3 %copy-start.43 = (s32[512]{0:T(512)S(1)}, s32[512]{0:T(512)}, u32[]{:S(2)}) copy-start(s32[512]{0:T(512)} %slice.137) | copy-start | bytes 6148
  97.4 16.3 %copy-start.44 = (s32[512]{0:T(512)S(1)}, s32[512]{0:T(512)}, u32[]{:S(2)}) copy-start(s32[512]{0:T(512)} %get-tuple-element.95) | copy-start | bytes 6148
  97.4 16.8 %copy-start.13 = (bf16[1,512,192]{1,2,0:T(8,128)(2,1)S(1)}, bf16[1,512,192]{1,2,0:T(8,128)(2,1)}, u32[]{:S(2)}) copy-start(bf16[1,512,192]{1,2,0:T(8,128)(2,1)} %get-tuple-element.88) | copy-start | bytes 589828
  97.4 16.8 %copy-start.15 = (bf16[1,512,192]{1,2,0:T(8,128)(2,1)S(1)}, bf16[1,512,192]{1,2,0:T(8,128)(2,1)}, u32[]{:S(2)}) copy-start(bf16[1,512,192]{1,2,0:T(8,128)(2,1)} %get-tuple-element.86) | copy-start | bytes 589828
  117.1 6.3 copy-start.2
  127.2 61.6 %all-gather.6.cloned.1.call-start = ((), (), s32[]{:S(2)}) async-start(), calls=%async_computation.1 | async-start | bytes 1474560 | tf_op jit(solution)/shard_map/all_gather | solution.py:914
  127.9 428.5 %all-reduce.9.cloned.1.call-start = ((), (), s32[]{:S(2)}) async-start(), calls=%async_computation.3 | async-start | bytes 6291456 | tf_op jit(solution)/shard_map/psum | solution.py:1009
  307.4 15.3 %copy-start.17 = (bf16[512,192]{0,1:T(8,128)(2,1)S(1)}, bf16[512,192]{0,1:T(8,128)(2,1)}, u32[]{:S(2)}) copy-start(bf16[512,192]{0,1:T(8,128)(2,1)} %get-tuple-element.93) | copy-start | bytes 589828
  332.3 47.5 %copy-start.20 = (f32[512,3,64]{0,2,1:T(8,128)S(1)}, f32[512,3,64]{0,2,1:T(8,128)}, u32[]{:S(2)}) copy-start(f32[512,3,64]{0,2,1:T(8,128)} %fusion.45) | copy-start | bytes 1179652
  414.2 7.2 %copy-start.26 = (bf16[1024,3,64]{0,2,1:T(8,128)(2,1)}, bf16[1024,3,64]{0,2,1:T(8,128)(2,1)S(1)}, u32[]{:S(2)}) copy-start(bf16[1024,3,64]{0,2,1:T(8,128)(2,1)S(1)} %fusion.41) | copy-start | bytes 1179652
  414.7 6.7 %copy-start.24 = (bf16[512,3,64]{0,2,1:T(8,128)(2,1)S(1)}, bf16[512,3,64]{0,2,1:T(8,128)(2,1)}, u32[]{:S(2)}) copy-start(bf16[512,3,64]{0,2,1:T(8,128)(2,1)} %fusion.55) | copy-start | bytes 589828
  414.7 6.7 %copy-start.25 = (bf16[512,3,64]{0,2,1:T(8,128)(2,1)S(1)}, bf16[512,3,64]{0,2,1:T(8,128)(2,1)}, u32[]{:S(2)}) copy-start(bf16[512,3,64]{0,2,1:T(8,128)(2,1)} %fusion.56) | copy-start | bytes 589828
  414.7 6.7 %copy-start.29 = (bf16[1024,3,64]{0,2,1:T(8,128)(2,1)S(1)}, bf16[1024,3,64]{0,2,1:T(8,128)(2,1)}, u32[]{:S(2)}) copy-start(bf16[1024,3,64]{0,2,1:T(8,128)(2,1)} %fusion.42) | copy-start | bytes 1179652
  424.7 227.9 %all-reduce.11.cloned.1.call-start = ((), (), s32[]{:S(2)}) async-start(), calls=%async_computation.4 | async-start | bytes 4718592 | tf_op jit(solution)/shard_map/psum | solution.py:1012
  424.7 8.8 %copy-start.47 = (s32[1023]{0:T(1024)S(1)}, s32[1023]{0:T(1024)}, u32[]{:S(2)}) copy-start(s32[1023]{0:T(1024)} %copy-done.46) | copy-start | bytes 12280
  434.4 64.2 %copy-start.41 = (f32[8,1,384]{2,1,0:T(1,128)S(1)}, f32[8,1,384]{2,1,0:T(1,128)}, u32[]{:S(2)}) copy-start(f32[8,1,384]{2,1,0:T(1,128)} %get-tuple-element.34) | copy-start | bytes 36868
  527.6 6.2 copy-start.8
  527.6 6.2 copy-start.27
  (37 other events, 117.4 us)
Sparse Core Ops, SparseCore 0:
  9.6 22.3 all-gather.7
  127.3 22.3 all-gather.3
  151.2 26.0 all-gather.5
  424.8 80.0 all-reduce.8
  546.0 106.5 all-reduce.10
